TPU v7x, 32 devices: a whole 2x2x4 slice. The times are simulated.
32 devices in a mesh: parts: 2 (over x), sta: 16 (over z, y, core).
Axes of the slice: x: 2, y: 2, z: 4, core: 2. Of those that a mesh axis runs over, the one named last changes fastest.
Arguments:
- raw_traces: bfloat16 [512, 16384], P('parts', 'sta'), parts along dimension 0, may hold values from -6 to 6
- filter_taps: bfloat16 [256], replicated, may hold values from -0.375 to 0.375
- station_order: int32 [512], P('parts'), parts along dimension 0, may hold values from 0 to 255, each once
- window_starts: int32 [32], P('parts'), parts along dimension 0, may hold values from 0 to 2048, as said below
- pairing: int32 [4, 16], replicated, may hold values from 0 to 15, as said below
Outputs:
- correlation: float32 [4, 512, 16, 256], P(None, ('parts', 'sta')), parts along dimension 1
There are 2 independent parts, one for each index of `parts`. A program takes and returns all parts, laid end to end along the dimension named above; an argument that names none is the same for every part. Nothing has to cross between parts.
Inputs may be any that keep to these rules, and one draw needn't show every extreme that they name: Each station appears once; block b holds the stations station_order[b * 16 + j], j < 16. `window_starts`: starts never fall; the first is 0 and the last is 2048; consecutive starts differ by at most 273. Row r is one round of a single round-robin tournament over the 16 blocks: pairing[r, pairing[r, b]] = b, pairing[r, b] != b, and no two rows pair the same two blocks.
All inputs are finite; a program needn't handle non-finite values.
Results may differ from a plain program's by a relative error of at most 0.0049.
Values may be sent and summed in bfloat16 or wider, within the bound.
A program may use at most 128 MiB of HBM per device.

v0:
```python
import math

import jax
import jax.numpy as jnp
from jax import lax
from jax.sharding import PartitionSpec as P

DEC = 4
TAPS = 256
SEG = 2048
BAND = 64
LAGS = 256
ROUNDS = 4
BINS = 1024


def decimate(signal, leading, filter_taps, factor):
    row_count, length = signal.shape
    outputs = length // factor
    per_tile = math.gcd(outputs, 128)
    tile_span = per_tile * factor
    margin = leading.shape[1]
    pieces = 1 + (margin + tile_span - 1) // tile_span
    tile_count = outputs // per_tile
    padded = jnp.concatenate(
        [leading, signal, jnp.zeros((row_count, (pieces - 1) * tile_span - margin), signal.dtype)],
        axis=1,
    )
    tap_count = filter_taps.shape[0]
    positions = jnp.arange(pieces * tile_span, dtype=jnp.int32)[:, None]
    column = jnp.arange(per_tile, dtype=jnp.int32)[None, :]
    tap_index = column * factor + tap_count - 1 - positions
    inside = (tap_index >= 0) & (tap_index < tap_count)
    banded = jnp.where(
        inside,
        jnp.take(filter_taps, jnp.clip(tap_index, 0, tap_count - 1)),
        jnp.zeros((), filter_taps.dtype),
    )
    summed = jnp.zeros((row_count, tile_count, per_tile), jnp.float32)
    for section_index in range(pieces):
        segment = padded[:, section_index * tile_span : section_index * tile_span + length].reshape(
            row_count, tile_count, tile_span
        )
        summed = summed + jnp.einsum(
            "rtu,ui->rti",
            segment,
            banded[section_index * tile_span : (section_index + 1) * tile_span],
            preferred_element_type=jnp.float32,
        )
    return summed.reshape(row_count, outputs)


def dft_matrix(seg_length, bin_count):
    sample = jnp.arange(seg_length, dtype=jnp.int32)
    frequency = jnp.arange(bin_count, dtype=jnp.int32)
    angles = (frequency[:, None] * sample[None, :] % seg_length).astype(jnp.float32) * (
        2.0 * math.pi / seg_length
    )
    taper_curve = 0.5 - 0.5 * jnp.cos(sample.astype(jnp.float32) * (2.0 * math.pi / seg_length))
    joined = jnp.concatenate(
        [jnp.cos(angles) * taper_curve[None, :], -jnp.sin(angles) * taper_curve[None, :]], axis=0
    )
    return joined.astype(jnp.bfloat16)


def lag_matrix(seg_length, bin_count, lag_count, window_count):
    frequency = jnp.arange(bin_count, dtype=jnp.int32)
    lag_offset = jnp.arange(lag_count, dtype=jnp.int32) - lag_count // 2 + seg_length
    angles = (frequency[:, None] * lag_offset[None, :] % seg_length).astype(jnp.float32) * (
        2.0 * math.pi / seg_length
    )
    normalizer = 1.0 / math.sqrt(bin_count * window_count)
    return jnp.stack([jnp.cos(angles) * normalizer, -jnp.sin(angles) * normalizer]).astype(
        jnp.bfloat16
    )


def whiten_flat(spectrum, band_width):
    halves, bin_count, columns = spectrum.shape
    grouped = spectrum.reshape(halves, bin_count // band_width, band_width, columns)
    band_level = jnp.sum(grouped * grouped, axis=(0, 2)) / (2 * band_width)
    scaled = grouped * (1.0 / jnp.sqrt(band_level + 1e-06))[None, :, None]
    return scaled.reshape(spectrum.shape).astype(jnp.bfloat16)


def cross_spectra(left_spec, right_spec):
    turned = jnp.stack([right_spec, jnp.stack([-right_spec[1], right_spec[0]])])
    return jnp.einsum("cfws,kcfwt->kfst", left_spec, turned, preferred_element_type=jnp.float32)


def body(raw_traces, filter_taps, station_order, window_starts, pairing):
    members = lax.axis_size("sta")
    station_count, local_time = raw_traces.shape
    block_size = station_count // members
    margin = TAPS - DEC
    ordered = jnp.take(raw_traces, station_order, axis=0)
    gathered = lax.all_to_all(ordered, "sta", split_axis=0, concat_axis=1, tiled=True)
    leading = jnp.zeros((block_size, margin), gathered.dtype)
    low_rate = decimate(gathered, leading, filter_taps, DEC).astype(jnp.bfloat16)
    window_count = window_starts.shape[0]
    windows = jax.vmap(
        lambda first_sample: lax.dynamic_slice_in_dim(low_rate, first_sample, SEG, 1)
    )(window_starts)
    windows = windows.reshape(window_count * block_size, SEG)
    spectrum = lax.dot_general(
        dft_matrix(SEG, BINS), windows, (((1,), (1,)), ((), ())), preferred_element_type=jnp.float32
    )
    whitened = whiten_flat(spectrum.reshape(2, BINS, window_count * block_size), BAND)
    by_bin = lax.all_to_all(whitened[None], "sta", split_axis=2, concat_axis=0, tiled=True)
    lag_table = lag_matrix(SEG, BINS, LAGS, window_count)
    own_spec = whitened.reshape(2, BINS, window_count, block_size)
    collected = []
    for round_index in range(ROUNDS):
        picked = jnp.take(by_bin, pairing[round_index], axis=0)
        partner_spec = lax.all_to_all(picked, "sta", split_axis=0, concat_axis=2, tiled=True)
        partner_spec = partner_spec.reshape(2, BINS, window_count, block_size)
        cross_spec = cross_spectra(own_spec, partner_spec).astype(jnp.bfloat16)
        collected.append(cross_spec.reshape(2, BINS, block_size * block_size))
    correlated = jnp.einsum(
        "rkfp,kfl->rpl", jnp.stack(collected), lag_table, preferred_element_type=jnp.float32
    )
    return correlated.reshape(ROUNDS, block_size, block_size, LAGS)


def solution(mesh):
    return jax.shard_map(
        body,
        mesh=mesh,
        in_specs=(P("parts", "sta"), P(), P("parts"), P("parts"), P()),
        out_specs=P(None, ("parts", "sta"), None, None),
        check_vma=False,
    )
```

profile of v0, /device:TPU:0, one launch (start us, length us, event | category | flops | bytes accessed | tf_op | source)
XLA Modules:
  0.0 1280.5 jit_solution(12925101330786375420)
XLA Ops:
  3.6 7.4 all-to-all-start
  11.3 35.5 %multiply_convert_fusion.1 = (bf16[1024,2048]{1,0:T(8,128)(2,1)}, bf16[1024,2048]{1,0:T(8,128)(2,1)}) fusion(f32[2048]{0:T(1024)S(1)} %multiply_subtract_fusion), kind=kLoop, calls=%fused_computation.20 | loop fusion | flops 39845888 | bytes 8396800 | tf_op jit(solution)/shard_map/convert.2
  46.8 764.8 %gather_fusion.1 = bf16[131072]{0:T(1024)(128)(2,1)S(1)} fusion(bf16[256]{0:T(256)(128)(2,1)S(1)} %copy-done.2, s32[131072]{0:T(1024)S(1)} %fusion.28), kind=kCustom, calls=%fused_computation.5 | custom fusion | bytes 1048576 | tf_op jit(solution)/shard_map/jit(_take)/gather | solution.py:36
  812.0 8.4 pad_maximum_fusion
  821.7 21.5 %while.1 = (s32[]{:T(128)}, bf16[16,4096]{1,0:T(8,128)(2,1)S(1)}, s32[16,2]{0,1:T(2,128)S(1)}, bf16[16,16,2048]{2,1,0:T(8,128)(2,1)S(1)}, s32[]{:T(128)}) while((s32[]{:T(128)}, bf16[16,4096]{1,0:T(8,128)(2,1)S(1)}, s32[16,2]{0,1:T(2,128)S(1)}, bf16[16,16,2048]{2,1,0:T(8,128)(2,1)S(1)}, s32[]{:T(128)}) %tuple.38), condition=%wide.while_cond, body=%wide.while_body.sunk | while | flops 2 | bytes 131169 | solution.py:102
  857.5 22.9 %all-to-all-done.1 = bf16[1,2,1024,256]{3,1,0,2:T(2,128)(2,1)S(1)} async-done(((bf16[1,2,1024,256]{3,1,0,2:T(2,128)(2,1)}), bf16[1,2,1024,256]{3,1,0,2:T(2,128)(2,1)S(1)}, u32[]{:S(2)}, u32[]{:S(2)}) %all-to-all-start.1) | async-done | bytes 1048608 | tf_op jit(solution)/shard_map/all_to_all | solution.py:109
  897.6 19.0 %all-to-all-done.2 = bf16[16,2,64,256]{3,2,1,0:T(8,128)(2,1)} async-done(((bf16[16,2,64,256]{3,2,1,0:T(8,128)(2,1)}), bf16[16,2,64,256]{3,2,1,0:T(8,128)(2,1)}, u32[]{:S(2)}, u32[]{:S(2)}) %all-to-all-start.2) | async-done | bytes 1048608 | tf_op jit(solution)/shard_map/all_to_all | solution.py:115
  916.6 7.2 all-to-all-start.3
  927.7 19.0 %all-to-all-done.3 = bf16[16,2,64,256]{3,2,1,0:T(8,128)(2,1)} async-done(((bf16[16,2,64,256]{3,2,1,0:T(8,128)(2,1)}), bf16[16,2,64,256]{3,2,1,0:T(8,128)(2,1)}, u32[]{:S(2)}, u32[]{:S(2)}) %all-to-all-start.3) | async-done | bytes 1048608 | tf_op jit(solution)/shard_map/all_to_all | solution.py:115
  946.8 6.9 all-to-all-start.4
  957.6 19.0 %all-to-all-done.4 = bf16[16,2,64,256]{3,2,1,0:T(8,128)(2,1)} async-done(((bf16[16,2,64,256]{3,2,1,0:T(8,128)(2,1)}), bf16[16,2,64,256]{3,2,1,0:T(8,128)(2,1)}, u32[]{:S(2)}, u32[]{:S(2)}) %all-to-all-start.4) | async-done | bytes 1048608 | tf_op jit(solution)/shard_map/all_to_all | solution.py:115
  995.1 12.1 copy.132
  1036.3 32.0 %copy.110 = bf16[2,2,1024,16,16]{3,4,1,0,2:T(8,128)(2,1)} copy(bf16[2,2,1024,16,16]{2,4,3,1,0:T(8,128)(2,1)S(1)} %pad_maximum_fusion.1) | data formatting | bytes 4194304 | tf_op jit(solution)/shard_map/stack | solution.py:87
  1068.3 13.4 %fusion.6 = bf16[2,1024,16,16]{2,3,0,1:T(8,128)(2,1)} fusion(bf16[2,2,1024,16,16]{3,4,1,0,2:T(8,128)(2,1)} %copy.110, bf16[2,1024,16,16,1]{3,2,0,4,1:T(8,128)(2,1)} %copy.132), kind=kOutput, calls=%fused_computation.24 | convolution fusion | flops 34078720 | bytes 4194304 | tf_op jit(solution)/shard_map/cfws,kcfwt->kfst/dot_general | solution.py:88
  1081.7 10.1 copy.112
  1107.8 23.2 %copy.116 = bf16[2,2,1024,16,16]{3,4,1,0,2:T(8,128)(2,1)} copy(bf16[2,2,1024,16,16]{2,4,3,1,0:T(8,128)(2,1)S(1)} %pad_maximum_fusion.2) | data formatting | bytes 4194304 | tf_op jit(solution)/shard_map/stack | solution.py:87
  1131.1 13.4 %fusion.7 = bf16[2,1024,16,16]{2,3,0,1:T(8,128)(2,1)} fusion(bf16[2,2,1024,16,16]{3,4,1,0,2:T(8,128)(2,1)} %copy.116, bf16[2,1024,16,16,1]{3,2,0,4,1:T(8,128)(2,1)} %copy.132), kind=kOutput, calls=%fused_computation.25 | convolution fusion | flops 34078720 | bytes 4194304 | tf_op jit(solution)/shard_map/cfws,kcfwt->kfst/dot_general | solution.py:88
  1144.5 10.3 copy.118
  1170.8 23.2 %copy.122 = bf16[2,2,1024,16,16]{3,4,1,0,2:T(8,128)(2,1)} copy(bf16[2,2,1024,16,16]{2,4,3,1,0:T(8,128)(2,1)S(1)} %pad_maximum_fusion.3) | data formatting | bytes 4194304 | tf_op jit(solution)/shard_map/stack | solution.py:87
  1194.0 13.4 %fusion.8 = bf16[2,1024,16,16]{2,3,0,1:T(8,128)(2,1)} fusion(bf16[2,2,1024,16,16]{3,4,1,0,2:T(8,128)(2,1)} %copy.122, bf16[2,1024,16,16,1]{3,2,0,4,1:T(8,128)(2,1)} %copy.132), kind=kOutput, calls=%fused_computation.26 | convolution fusion | flops 34078720 | bytes 4194304 | tf_op jit(solution)/shard_map/cfws,kcfwt->kfst/dot_general | solution.py:88
  1207.4 10.2 copy.124
  1229.2 23.2 %copy.128 = bf16[2,2,1024,16,16]{3,4,1,0,2:T(8,128)(2,1)} copy(bf16[2,2,1024,16,16]{2,4,3,1,0:T(8,128)(2,1)S(1)} %pad_maximum_fusion.4) | data formatting | bytes 4194304 | tf_op jit(solution)/shard_map/stack | solution.py:87
  1252.5 13.4 %fusion.9 = bf16[2,1024,16,16]{2,3,0,1:T(8,128)(2,1)} fusion(bf16[2,2,1024,16,16]{3,4,1,0,2:T(8,128)(2,1)} %copy.128, bf16[2,1024,16,16,1]{3,2,0,4,1:T(8,128)(2,1)} %copy.132), kind=kOutput, calls=%fused_computation.27 | convolution fusion | flops 34078720 | bytes 4194304 | tf_op jit(solution)/shard_map/cfws,kcfwt->kfst/dot_general | solution.py:88
  1265.9 10.1 copy.130
  (156 shorter events, 161.0 us)
Async XLA Ops:
  0.0 1.5 copy-start
  0.0 46.8 %copy-start.11 = (s32[16]{0:T(128)S(1)}, s32[16]{0:T(128)}, u32[]{:S(2)}) copy-start(s32[16]{0:T(128)} %param.10) | copy-start | bytes 196
  0.0 46.8 %copy-start.2 = (bf16[256]{0:T(256)(128)(2,1)S(1)}, bf16[256]{0:T(256)(128)(2,1)}, u32[]{:S(2)}) copy-start(bf16[256]{0:T(256)(128)(2,1)} %param.8) | copy-start | bytes 1540
  3.6 816.7 %all-to-all-start = ((bf16[16,16,1024]{2,1,0:T(8,128)(2,1)}), bf16[16,16,1024]{2,1,0:T(8,128)(2,1)S(1)}, u32[]{:S(2)}, u32[]{:S(2)}) async-start(bf16[16,16,1024]{2,1,0:T(8,128)(2,1)} %broadcast_select_fusion.4), calls=%async_computation | async-start | bytes 1048576 | tf_op jit(solution)/shard_map/all_to_all | solution.py:97
  843.3 14.2 %copy-start.10 = (s32[4,16]{1,0:T(4,128)S(1)}, s32[4,16]{1,0:T(4,128)}, u32[]{:S(2)}) copy-start(s32[4,16]{1,0:T(4,128)} %param.11) | copy-start | bytes 772
  851.4 29.0 %all-to-all-start.1 = ((bf16[1,2,1024,256]{3,1,0,2:T(2,128)(2,1)}), bf16[1,2,1024,256]{3,1,0,2:T(2,128)(2,1)S(1)}, u32[]{:S(2)}, u32[]{:S(2)}) async-start(bf16[1,2,1024,256]{3,1,0,2:T(2,128)(2,1)} %copy.103), calls=%async_computation.1 | async-start | bytes 2097152 | tf_op jit(solution)/shard_map/all_to_all | solution.py:109
  880.4 1.0 copy-start.6
  886.7 29.9 %all-to-all-start.2 = ((bf16[16,2,64,256]{3,2,1,0:T(8,128)(2,1)}), bf16[16,2,64,256]{3,2,1,0:T(8,128)(2,1)}, u32[]{:S(2)}, u32[]{:S(2)}) async-start(bf16[16,2,64,256]{3,2,1,0:T(8,128)(2,1)} %broadcast_select_fusion.3), calls=%async_computation.2 | async-start | bytes 2097152 | tf_op jit(solution)/shard_map/all_to_all | solution.py:115
  916.6 30.2 %all-to-all-start.3 = ((bf16[16,2,64,256]{3,2,1,0:T(8,128)(2,1)}), bf16[16,2,64,256]{3,2,1,0:T(8,128)(2,1)}, u32[]{:S(2)}, u32[]{:S(2)}) async-start(bf16[16,2,64,256]{3,2,1,0:T(8,128)(2,1)} %broadcast_select_fusion.2), calls=%async_computation.3 | async-start | bytes 2097152 | tf_op jit(solution)/shard_map/all_to_all | solution.py:115
  946.8 29.9 %all-to-all-start.4 = ((bf16[16,2,64,256]{3,2,1,0:T(8,128)(2,1)}), bf16[16,2,64,256]{3,2,1,0:T(8,128)(2,1)}, u32[]{:S(2)}, u32[]{:S(2)}) async-start(bf16[16,2,64,256]{3,2,1,0:T(8,128)(2,1)} %broadcast_select_fusion.1), calls=%async_computation.4 | async-start | bytes 2097152 | tf_op jit(solution)/shard_map/all_to_all | solution.py:115
  976.7 47.8 %all-to-all-start.5 = ((bf16[16,2,64,256]{3,2,1,0:T(8,128)(2,1)}), bf16[16,2,64,256]{3,2,1,0:T(8,128)(2,1)S(1)}, u32[]{:S(2)}, u32[]{:S(2)}) async-start(bf16[16,2,64,256]{3,2,1,0:T(8,128)(2,1)} %broadcast_select_fusion), calls=%async_computation.5 | async-start | bytes 2097152 | tf_op jit(solution)/shard_map/all_to_all | solution.py:115
  1081.7 21.1 %copy-start.5 = (bf16[1,2,16,64,256]{3,2,4,1,0:T(8,128)(2,1)S(1)}, bf16[1,2,16,64,256]{3,2,4,1,0:T(8,128)(2,1)}, u32[]{:S(2)}) copy-start(bf16[1,2,16,64,256]{3,2,4,1,0:T(8,128)(2,1)} %copy.113) | copy-start | bytes 3145732
  1144.5 21.3 %copy-start.4 = (bf16[1,2,16,64,256]{3,2,4,1,0:T(8,128)(2,1)S(1)}, bf16[1,2,16,64,256]{3,2,4,1,0:T(8,128)(2,1)}, u32[]{:S(2)}) copy-start(bf16[1,2,16,64,256]{3,2,4,1,0:T(8,128)(2,1)} %copy.119) | copy-start | bytes 3145732
  1207.4 17.8 %copy-start.3 = (bf16[1,2,16,64,256]{3,2,4,1,0:T(8,128)(2,1)S(1)}, bf16[1,2,16,64,256]{3,2,4,1,0:T(8,128)(2,1)}, u32[]{:S(2)}) copy-start(bf16[1,2,16,64,256]{3,2,4,1,0:T(8,128)(2,1)} %copy.125) | copy-start | bytes 3145732
  1265.9 10.1 copy-start.7
  1265.9 10.1 copy-start.8
  1265.9 10.1 copy-start.9
  1276.0 4.0 copy-start.1
where the time goes:
time: 1290 us; the launch traced here: 1280 us
  local copies, waits for them, and re-layouts  1020 us (79%)
  waiting for transfers between devices  80 us (6%)
  other arithmetic  76.3 us (6%)
  matrix products  64.1 us (5%)
  starting transfers between devices  41.3 us (3%)
    gather x1, local copies, waits for them, and re-layouts, decimate(): jnp.take(filter_taps, jnp.clip(tap_index, 0, tap_count - 1))  765 us
    another operation x8, local copies, waits for them, and re-layouts, cross_spectra(): turned = jnp.stack([right_spec, jnp.stack([-right_spec[1], right_spec[0]])])  113 us
    all_to_all x4, waiting for transfers between devices, body(): lax.all_to_all(picked, 'sta', split_axis=0, concat_axis=2, tiled=True)  57.1 us
    dot_general x4, matrix products, cross_spectra(): jnp.einsum('cfws,kcfwt->kfst', left_spec, turned, preferred_element_type=...  53.7 us
    another operation x2, other arithmetic  41 us
    convert_element_type x4, local copies, waits for them, and re-layouts, body(): cross_spec = cross_spectra(own_spec, partner_spec).astype(jnp.bfloat16)  40.7 us
    all_to_all x4, starting transfers between devices, body(): lax.all_to_all(picked, 'sta', split_axis=0, concat_axis=2, tiled=True)  27.9 us
  transfers between devices with their start and end apart: 6, of which 4 were waited for; matrix products, arithmetic and copies ran while one was open for 67% of the time, Pallas kernels for 0%

commit v1 on v0

v1 whole, which is shorter than its diff:
```python
import functools
import math

import jax
import jax.numpy as jnp
import ml_dtypes
import numpy as np
from jax import lax
from jax.experimental import pallas as pl
from jax.experimental.pallas import tpu as pltpu
from jax.sharding import PartitionSpec as P

SB = 16
DEC = 4
TAPS = 256
SEG = 2048
BAND = 64
LAGS = 256
ROUNDS = 4
BINS = 1024
LANE = 128
SPAN = LANE * DEC + TAPS
GROUPS = ROUNDS + 1
ROWS = GROUPS * SB
FT = 128
TILES = BINS // FT


def dft_tiles():
    sample = np.arange(SEG)
    frequency = np.arange(BINS)
    angles = (sample[:, None] * frequency[None, :] % SEG) * (2.0 * math.pi / SEG)
    taper = (0.5 - 0.5 * np.cos(sample * (2.0 * math.pi / SEG)))[:, None]
    both = np.stack([np.cos(angles) * taper, -np.sin(angles) * taper], axis=1)
    both = both.reshape(SEG, 2, TILES, FT).transpose(2, 0, 1, 3).reshape(TILES, SEG, 2 * FT)
    return both.astype(np.float32).astype(ml_dtypes.bfloat16)


def lag_tiles(window_count):
    frequency = np.arange(BINS)
    offset = np.arange(LAGS) - LAGS // 2 + SEG
    angles = (frequency[:, None] * offset[None, :] % SEG) * (2.0 * math.pi / SEG)
    scale = 1.0 / math.sqrt(BINS * window_count)
    both = np.stack([np.cos(angles) * scale, -np.sin(angles) * scale])
    both = both.reshape(2, TILES, FT, LAGS).transpose(1, 0, 2, 3).reshape(TILES, 2 * FT, LAGS)
    return both.astype(np.float32).astype(ml_dtypes.bfloat16)


def band_ones():
    same = np.arange(FT)[:, None] // BAND == np.arange(FT)[None, :] // BAND
    return np.concatenate([same, same]).astype(ml_dtypes.bfloat16)


def filter_kernel(raw_ref, halo_ref, taps_ref, order_ref, low_ref):
    stations = raw_ref.shape[0]
    banded = jnp.broadcast_to(taps_ref[...], (LANE, SPAN))
    banded = pltpu.roll(banded, 0, 1, stride=DEC, stride_axis=0).astype(jnp.bfloat16)
    picks = (lax.broadcasted_iota(jnp.int32, (stations, stations), 1) == order_ref[...]).astype(
        jnp.float32
    ).astype(jnp.bfloat16)
    dims = (((1,), (1,)), ((), ()))
    pieces = raw_ref.shape[1] // (LANE * DEC)
    for piece in range(pieces):
        first = piece * LANE * DEC - TAPS
        if piece == 0:
            samples = jnp.concatenate([halo_ref[...], raw_ref[:, : LANE * DEC]], axis=1)
        else:
            samples = raw_ref[:, first : first + SPAN]
        low = lax.dot_general(samples, banded, dims, preferred_element_type=jnp.float32)
        ordered = jnp.dot(picks, low.astype(jnp.bfloat16), preferred_element_type=jnp.float32)
        low_ref[piece] = ordered.astype(jnp.bfloat16)


def correlate_kernel(
    starts_ref, groups_ref, low_ref, dft_ref, lag_ref, ones_ref, out_ref, rows, windows, white, cross, sems
):
    tile = pl.program_id(0)
    planes = low_ref.shape[0]
    window_count = starts_ref.shape[0]

    @pl.when(tile == 0)
    def _():
        copies = []
        for g in range(GROUPS):
            first = pl.multiple_of(groups_ref[g] * SB, SB)
            copy = pltpu.make_async_copy(
                low_ref.at[:, pl.ds(first, SB), :],
                rows.at[pl.ds(0, planes), pl.ds(g * SB, SB), :],
                sems.at[g],
            )
            copy.start()
            copies.append(copy)
        rows[planes] = jnp.zeros((ROWS, LANE), jnp.bfloat16)
        for copy in copies:
            copy.wait()
        lane = lax.broadcasted_iota(jnp.int32, (ROWS, LANE), 1)

        def one_window(w, carry):
            start = starts_ref[w]
            plane = start // LANE
            left = LANE - start % LANE
            back = left % LANE
            now = pltpu.roll(rows[plane].astype(jnp.float32), back, 1)
            for piece in range(SEG // LANE):
                later = pltpu.roll(rows[plane + piece + 1].astype(jnp.float32), back, 1)
                windows[
                    pl.ds(pl.multiple_of(w * ROWS, SB), ROWS), piece * LANE : (piece + 1) * LANE
                ] = jnp.where(lane < left, now, later).astype(jnp.bfloat16)
                now = later
            return carry

        lax.fori_loop(0, window_count, one_window, 0)
        out_ref[...] = jnp.zeros_like(out_ref)

    per_chunk = 4

    def one_chunk(n, carry):
        chunk = windows[pl.ds(pl.multiple_of(n * per_chunk * ROWS, SB), per_chunk * ROWS), :]
        spectrum = jnp.dot(chunk, dft_ref[0], preferred_element_type=jnp.float32)
        real, imag = spectrum[:, :FT], spectrum[:, FT:]
        power = real * real + imag * imag
        high = power.astype(jnp.bfloat16)
        low = (power - high.astype(jnp.float32)).astype(jnp.bfloat16)
        level = jnp.dot(
            jnp.concatenate([high, low], axis=1), ones_ref[...], preferred_element_type=jnp.float32
        )
        scale = lax.rsqrt(level * (1.0 / (2 * BAND)) + 1e-06)
        for c, part in enumerate((real, imag)):
            rounded = (part * scale).astype(jnp.bfloat16).astype(jnp.float32)
            white[c, pl.ds(n * per_chunk, per_chunk)] = rounded.reshape(per_chunk, ROWS, FT)
        return carry

    lax.fori_loop(0, window_count // per_chunk, one_chunk, 0)

    pair = 2

    def one_pair(n, carry):
        re = [[jnp.zeros((SB, FT), jnp.float32)] * ROUNDS for _ in range(pair)]
        im = [[jnp.zeros((SB, FT), jnp.float32)] * ROUNDS for _ in range(pair)]
        for w in range(window_count):
            own = [
                [
                    jnp.broadcast_to(white[c, w, pl.ds(n * pair + p, 1), :], (SB, FT))
                    for c in range(2)
                ]
                for p in range(pair)
            ]
            for r in range(ROUNDS):
                theirs = [white[c, w, (r + 1) * SB : (r + 2) * SB, :] for c in range(2)]
                for p in range(pair):
                    re[p][r] = re[p][r] + own[p][0] * theirs[0] + own[p][1] * theirs[1]
                    im[p][r] = im[p][r] + own[p][1] * theirs[0] - own[p][0] * theirs[1]
        for p in range(pair):
            for r in range(ROUNDS):
                at = pl.ds(pl.multiple_of((n * pair + p) * SB, SB), SB)
                cross[r, at, :FT] = re[p][r].astype(jnp.bfloat16)
                cross[r, at, FT:] = im[p][r].astype(jnp.bfloat16)
        return carry

    lax.fori_loop(0, SB // pair, one_pair, 0)
    for r in range(ROUNDS):
        out_ref[r] += jnp.dot(cross[r], lag_ref[0], preferred_element_type=jnp.float32)


def body(raw_traces, filter_taps, station_order, window_starts, pairing):
    members = lax.axis_size("sta")
    me = lax.axis_index("sta")
    stations, local_time = raw_traces.shape
    window_count = window_starts.shape[0]
    pieces = local_time // (LANE * DEC)
    halo = lax.ppermute(
        raw_traces[:, local_time - TAPS :], "sta", [(i, i + 1) for i in range(members - 1)]
    )
    taps = jnp.pad(filter_taps.astype(jnp.float32)[::-1], (DEC, SPAN - TAPS - DEC)).reshape(1, SPAN)
    low = pl.pallas_call(
        filter_kernel,
        out_shape=jax.ShapeDtypeStruct((pieces, stations, LANE), jnp.bfloat16),
        compiler_params=pltpu.CompilerParams(vmem_limit_bytes=40 * 2**20),
    )(raw_traces, halo, taps, station_order.reshape(stations, 1))
    low = lax.all_gather(low, "sta", axis=0, tiled=True)
    groups = jnp.concatenate([me[None].astype(jnp.int32), lax.dynamic_slice_in_dim(pairing, me, 1, 1)[:, 0]])
    planes = low.shape[0]
    grid_spec = pltpu.PrefetchScalarGridSpec(
        num_scalar_prefetch=2,
        grid=(TILES,),
        in_specs=[
            pl.BlockSpec(memory_space=pl.ANY),
            pl.BlockSpec((1, SEG, 2 * FT), lambda n, *_: (n, 0, 0)),
            pl.BlockSpec((1, 2 * FT, LAGS), lambda n, *_: (n, 0, 0)),
            pl.BlockSpec((2 * FT, FT), lambda n, *_: (0, 0)),
        ],
        out_specs=pl.BlockSpec((ROUNDS, SB * SB, LAGS), lambda n, *_: (0, 0, 0)),
        scratch_shapes=[
            pltpu.VMEM((planes + 1, ROWS, LANE), jnp.bfloat16),
            pltpu.VMEM((window_count * ROWS, SEG), jnp.bfloat16),
            pltpu.VMEM((2, window_count, ROWS, FT), jnp.float32),
            pltpu.VMEM((ROUNDS, SB * SB, 2 * FT), jnp.bfloat16),
            pltpu.SemaphoreType.DMA((GROUPS,)),
        ],
    )
    correlated = pl.pallas_call(
        correlate_kernel,
        grid_spec=grid_spec,
        out_shape=jax.ShapeDtypeStruct((ROUNDS, SB * SB, LAGS), jnp.float32),
        compiler_params=pltpu.CompilerParams(vmem_limit_bytes=48 * 2**20),
    )(
        window_starts,
        groups,
        low,
        jnp.asarray(dft_tiles()),
        jnp.asarray(lag_tiles(window_count)),
        jnp.asarray(band_ones()),
    )
    return correlated.reshape(ROUNDS, SB, SB, LAGS)


def solution(mesh):
    return jax.shard_map(
        body,
        mesh=mesh,
        in_specs=(P("parts", "sta"), P(), P("parts"), P("parts"), P()),
        out_specs=P(None, ("parts", "sta"), None, None),
        check_vma=False,
    )
```

time: 1290 us -> 121 us (0.09)
  local copies, waits for them, and re-layouts: 1020 us -> 8.09 us
  other arithmetic: 76.3 us -> 0.08 us
  matrix products: 64.1 us -> 0 us
  Pallas kernels: 0 us -> 50.7 us
  starting transfers between devices: 41.3 us -> 2.37 us
  waiting for transfers between devices: 80 us -> 46.2 us
    gather x54 -> x0, local copies, waits for them, and re-layouts: 793 us -> none  [the longest x1 765 us: decimate(): jnp.take(filter_taps, jnp.clip(tap_index, 0, tap_count - 1))]
    another operation x8 -> x0, local copies, waits for them, and re-layouts: 113 us -> none  [cross_spectra(): turned = jnp.stack([right_spec, jnp.stack([-right_spec[1], right_spec[0]])])]
    all_to_all x6 -> x0, waiting for transfers between devices: 80 us -> none  [the longest x4 57.1 us: body(): lax.all_to_all(picked, 'sta', split_axis=0, concat_axis=2, tiled=True)]
    dot_general x8 -> x0, matrix products: 64.1 us -> none  [the longest x4 53.7 us: cross_spectra(): jnp.einsum('cfws,kcfwt->kfst', left_spec, turned, preferred_element_type=...]
    convert_element_type x8 -> x0, local copies, waits for them, and re-layouts: 60.9 us -> none  [the longest x4 40.7 us: body(): cross_spec = cross_spectra(own_spec, partner_spec).astype(jnp.bfloat16)]
    pallas_call x0 -> x2, Pallas kernels: none -> 50.7 us  [the longest x1 49.1 us: body(): pl.pallas_call(correlate_kernel, grid_spec=grid_spec, out_shape=jax.Shape...]
    another operation x10 -> x0, other arithmetic: 49.4 us -> none
    all_gather x0 -> x1, waiting for transfers between devices: none -> 46.2 us  [body(): low = lax.all_gather(low, 'sta', axis=0, tiled=True)]
  transfers between devices with their start and end apart: 6 -> 2, of which waited for: 4 -> 1; matrix products, arithmetic and copies ran while one was open for 67% -> 2% of each run, Pallas kernels for 0% -> 0%
where the time goes in v1:
time: 121 us
  Pallas kernels  50.7 us (42%)
  waiting for transfers between devices  46.2 us (38%)
  between operations  13.5 us (11%)
  local copies, waits for them, and re-layouts  8.09 us (7%)
  starting transfers between devices  2.37 us (2%)
    pallas_call x1, Pallas kernels, body(): pl.pallas_call(correlate_kernel, grid_spec=grid_spec, out_shape=jax.Shape...  49.1 us
    all_gather x1, waiting for transfers between devices, body(): low = lax.all_gather(low, 'sta', axis=0, tiled=True)  46.2 us
    unnamed x12, local copies, waits for them, and re-layouts  5.35 us
  transfers between devices with their start and end apart: 2, of which 1 were waited for; matrix products, arithmetic and copies ran while one was open for 2% of the time, Pallas kernels for 0%

profile of v1, /device:TPU:0, one launch (start us, length us, event | category | flops | bytes accessed | tf_op | source)
XLA Modules:
  0.0 121.0 jit_solution(10640743083923139954)
XLA Ops:
  6.5 0.0 copy-start
  6.5 0.0 all-gather.2.cloned.1.call-start
  6.5 0.9 slice.3
  7.5 2.4 %collective-permute-start = (bf16[256,256]{1,0:T(8,128)(2,1)S(1)}, bf16[256,256]{1,0:T(8,128)(2,1)S(1)}, u32[]{:S(2)}, u32[]{:S(2)}) collective-permute-start(bf16[256,256]{1,0:T(8,128)(2,1)S(1)} %slice.3), channel_id=1, source_target_pairs={{0,1},{1,2},{2,3},{3,4},{4,5},{5,6},{6,7},{7,8},{8,9},{9,10},{10,1... | collective-permute-start | bytes 393224 | tf_op jit(solution)/shard_map/ppermute | solution.py:171
  9.8 0.7 rev.3
  10.6 0.1 pad.4
  10.7 0.8 copy.10.order_ref
  11.5 0.0 collective-permute-done.halo_ref
  11.5 0.0 copy-start.3
  11.5 1.0 copy-done.3
  12.5 1.7 %shard_map.82 = bf16[2,256,128]{2,1,0:T(8,128)(2,1)} custom-call(bf16[256,1024]{1,0:T(8,128)(2,1)S(1)} %copy-done.3, bf16[256,256]{1,0:T(8,128)(2,1)S(1)} %collective-permute-done.halo_ref, f32[1,768]{1,0:T(1,128)S(1)} %reshape.9.taps_ref, s32[256,1]{1,0:T(8,128)S(1)} %copy.10.order_ref), custom_call_target="tpu_custom_call" | custom-call | tf_op jit(solution)/shard_map/pallas_call | solution.py:175
  14.2 0.0 all-gather.2.cloned.1.call-update
  14.2 0.0 copy-done
  14.2 0.2 dynamic-slice_reduce_fusion
  14.4 0.1 pad_add_fusion.groups_ref
  14.5 46.2 %all-gather.2.cloned.1.call-done.low_ref = bf16[32,256,128]{2,1,0:T(8,128)(2,1)} async-done(((bf16[2,256,128]{2,1,0:T(8,128)(2,1)}), bf16[32,256,128]{2,1,0:T(8,128)(2,1)}) %all-gather.2.cloned.1.call-update) | async-done | bytes 2097168 | tf_op jit(solution)/shard_map/all_gather | solution.py:180
  60.7 0.0 copy-start.1
  60.7 1.6 %copy-done.1 = bf16[32,256,128]{2,1,0:T(8,128)(2,1)S(1)} copy-done((bf16[32,256,128]{2,1,0:T(8,128)(2,1)S(1)}, bf16[32,256,128]{2,1,0:T(8,128)(2,1)}, u32[]{:S(2)}) %copy-start.1) | copy-done | bytes 2097176
  62.3 0.0 copy-start.2
  62.3 1.2 %copy-done.2 = bf16[8,256,256]{2,1,0:T(8,128)(2,1)S(1)} copy-done((bf16[8,256,256]{2,1,0:T(8,128)(2,1)S(1)}, bf16[8,256,256]{2,1,0:T(8,128)(2,1)}, u32[]{:S(2)}) %copy-start.2) | copy-done | bytes 1048600
  63.5 0.0 copy-start.4
  63.5 0.8 copy-done.4
  64.4 0.7 copy-done.5
  65.0 49.1 %shard_map.83 = f32[4,256,256]{2,1,0:T(8,128)} custom-call(s32[16]{0:T(128)S(1)} %copy-done.5, s32[5]{0:T(128)S(1)} %pad_add_fusion.groups_ref, bf16[32,256,128]{2,1,0:T(8,128)(2,1)S(1)} %copy-done.1, bf16[8,2048,256]{2,1,0:T(8,128)(2,1)} %constant.16.clone.dft_ref, bf16[8,256,256]{2,1,0:T(8,128)(2,1)S(1)} %copy-done.2, bf16[256,128]{1,0:T(8,128)(2,1)S(1)} %copy-done.4), custom_call_target="tpu_custom_call" | custom-call | tf_op jit(solution)/shard_map/pallas_call | solution.py:201
  (2 shorter events, 0.0 us)
Async XLA Ops:
  6.5 7.7 %copy-start = (s32[4,16]{1,0:T(4,128)S(1)}, s32[4,16]{1,0:T(4,128)}, u32[]{:S(2)}) copy-start(s32[4,16]{1,0:T(4,128)} %param.12) | copy-start | bytes 772
  6.5 54.2 %all-gather.2.cloned.1.call-start = ((), (), s32[]{:S(2)}) async-start(), calls=%async_computation | async-start | bytes 2228224 | tf_op jit(solution)/shard_map/all_gather | solution.py:180
  7.5 4.0 %collective-permute-start = (bf16[256,256]{1,0:T(8,128)(2,1)S(1)}, bf16[256,256]{1,0:T(8,128)(2,1)S(1)}, u32[]{:S(2)}, u32[]{:S(2)}) collective-permute-start(bf16[256,256]{1,0:T(8,128)(2,1)S(1)} %slice.3), channel_id=1, source_target_pairs={{0,1},{1,2},{2,3},{3,4},{4,5},{5,6},{6,7},{7,8},{8,9},{9,10},{10,1... | collective-permute-start | bytes 393224 | tf_op jit(solution)/shard_map/ppermute | solution.py:171
  11.5 1.0 copy-start.3
  60.7 1.6 %copy-start.1 = (bf16[32,256,128]{2,1,0:T(8,128)(2,1)S(1)}, bf16[32,256,128]{2,1,0:T(8,128)(2,1)}, u32[]{:S(2)}) copy-start(bf16[32,256,128]{2,1,0:T(8,128)(2,1)} %all-gather.2.cloned.1.call-done.low_ref) | copy-start | bytes 6291460
  62.3 1.2 %copy-start.2 = (bf16[8,256,256]{2,1,0:T(8,128)(2,1)S(1)}, bf16[8,256,256]{2,1,0:T(8,128)(2,1)}, u32[]{:S(2)}) copy-start(bf16[8,256,256]{2,1,0:T(8,128)(2,1)} %constant.17.clone.lag_ref) | copy-start | bytes 3145732
  63.5 0.8 copy-start.4
  64.4 0.7 copy-start.5
Sparse Core Ops, SparseCore 0:
  14.3 46.3 all-gather.1

commit v2 on v1

--- a/solution.py
+++ b/solution.py
@@ -24,6 +24,8 @@
 ROWS = GROUPS * SB
 FT = 128
 TILES = BINS // FT
+QUAD = 4
+MESH = pl.DeviceIdType.MESH
 
 
 def dft_tiles():
@@ -51,24 +53,114 @@
     return np.concatenate([same, same]).astype(ml_dtypes.bfloat16)
 
 
-def filter_kernel(raw_ref, halo_ref, taps_ref, order_ref, low_ref):
-    stations = raw_ref.shape[0]
+def gather_kernel(members, raw_ref, taps_ref, order_ref, out_ref, halo, low, halo_sems, own_sem, send_sems, recv_sems):
+    me = lax.axis_index("sta")
+    stations, local_time = raw_ref.shape
+    line = members // QUAD
+    rank, lead = me // QUAD, me % QUAD
+    far = [lax.rem(rank + k, line) * QUAD + lead for k in range(1, line)]
+    across = rank * QUAD + lax.rem(lead + 2, QUAD)
+    twin = me + 1 - 2 * lax.rem(me, 2)
+    after, before = lax.rem(me + 1, members), lax.rem(me + members - 1, members)
+
+    barrier = pltpu.get_barrier_semaphore()
+    greeted = far + [across, twin, after, before]
+    for peer in greeted:
+        pl.semaphore_signal(barrier, inc=1, device_id={"sta": peer}, device_id_type=MESH)
+    pl.semaphore_wait(barrier, len(greeted))
+
+    halo_copy = pltpu.make_async_remote_copy(
+        src_ref=raw_ref.at[:, local_time - TAPS :],
+        dst_ref=halo,
+        send_sem=halo_sems.at[0],
+        recv_sem=halo_sems.at[1],
+        device_id={"sta": after},
+        device_id_type=MESH,
+    )
+
+    @pl.when(me < members - 1)
+    def _():
+        halo_copy.start()
+
     banded = jnp.broadcast_to(taps_ref[...], (LANE, SPAN))
     banded = pltpu.roll(banded, 0, 1, stride=DEC, stride_axis=0).astype(jnp.bfloat16)
     picks = (lax.broadcasted_iota(jnp.int32, (stations, stations), 1) == order_ref[...]).astype(
         jnp.float32
     ).astype(jnp.bfloat16)
     dims = (((1,), (1,)), ((), ()))
-    pieces = raw_ref.shape[1] // (LANE * DEC)
-    for piece in range(pieces):
+
+    def filtered(piece, samples):
+        summed = lax.dot_general(samples, banded, dims, preferred_element_type=jnp.float32)
+        ordered = jnp.dot(picks, summed.astype(jnp.bfloat16), preferred_element_type=jnp.float32)
+        low[piece] = ordered.astype(jnp.bfloat16)
+
+    for piece in range(1, low.shape[0]):
         first = piece * LANE * DEC - TAPS
-        if piece == 0:
-            samples = jnp.concatenate([halo_ref[...], raw_ref[:, : LANE * DEC]], axis=1)
-        else:
-            samples = raw_ref[:, first : first + SPAN]
-        low = lax.dot_general(samples, banded, dims, preferred_element_type=jnp.float32)
-        ordered = jnp.dot(picks, low.astype(jnp.bfloat16), preferred_element_type=jnp.float32)
-        low_ref[piece] = ordered.astype(jnp.bfloat16)
+        filtered(piece, raw_ref[:, first : first + SPAN])
+
+    @pl.when(me > 0)
+    def _():
+        halo_copy.wait_recv()
+
+    @pl.when(me == 0)
+    def _():
+        halo[...] = jnp.zeros_like(halo)
+
+    filtered(0, jnp.concatenate([halo[...], raw_ref[:, : LANE * DEC]], axis=1))
+
+    sent = []
+
+    def send(source, slot, peer):
+        n = len(sent)
+        copy = pltpu.make_async_remote_copy(
+            src_ref=source,
+            dst_ref=out_ref.at[slot],
+            send_sem=send_sems.at[n],
+            recv_sem=recv_sems.at[slot],
+            device_id={"sta": peer},
+            device_id_type=MESH,
+        )
+        copy.start()
+        sent.append(copy)
+
+    def arrived(slot):
+        pltpu.make_async_remote_copy(
+            src_ref=low,
+            dst_ref=out_ref.at[slot],
+            send_sem=send_sems.at[0],
+            recv_sem=recv_sems.at[slot],
+            device_id={"sta": twin},
+            device_id_type=MESH,
+        ).wait_recv()
+
+    order = sorted(range(line - 1), key=lambda k: min(k + 1, line - 1 - k))
+    for k in order:
+        send(low, me, far[k])
+    send(low, me, across)
+    send(low, me, twin)
+    own = pltpu.make_async_copy(low, out_ref.at[me], own_sem)
+    own.start()
+    shift = across - me
+    arrived(me + shift)
+    send(out_ref.at[me + shift], me + shift, twin)
+    for k in order:
+        arrived(far[k])
+        send(out_ref.at[far[k]], far[k], across)
+        send(out_ref.at[far[k]], far[k], twin)
+    for k in order:
+        arrived(far[k] + shift)
+        send(out_ref.at[far[k] + shift], far[k] + shift, twin)
+    turn = twin - me
+    for slot in [me] + [far[k] for k in order]:
+        arrived(slot + turn)
+        arrived(slot + shift + turn)
+    own.wait()
+    for copy in sent:
+        copy.wait_send()
+
+    @pl.when(me < members - 1)
+    def _():
+        halo_copy.wait_send()
 
 
 def correlate_kernel(
@@ -168,16 +260,26 @@
     stations, local_time = raw_traces.shape
     window_count = window_starts.shape[0]
     pieces = local_time // (LANE * DEC)
-    halo = lax.ppermute(
-        raw_traces[:, local_time - TAPS :], "sta", [(i, i + 1) for i in range(members - 1)]
-    )
     taps = jnp.pad(filter_taps.astype(jnp.float32)[::-1], (DEC, SPAN - TAPS - DEC)).reshape(1, SPAN)
+    in_vmem = pl.BlockSpec(memory_space=pltpu.VMEM)
     low = pl.pallas_call(
-        filter_kernel,
-        out_shape=jax.ShapeDtypeStruct((pieces, stations, LANE), jnp.bfloat16),
-        compiler_params=pltpu.CompilerParams(vmem_limit_bytes=40 * 2**20),
-    )(raw_traces, halo, taps, station_order.reshape(stations, 1))
-    low = lax.all_gather(low, "sta", axis=0, tiled=True)
+        functools.partial(gather_kernel, members),
+        out_shape=jax.ShapeDtypeStruct((members, pieces, stations, LANE), jnp.bfloat16),
+        in_specs=[in_vmem] * 3,
+        out_specs=pl.BlockSpec(memory_space=pl.ANY),
+        scratch_shapes=[
+            pltpu.VMEM((stations, TAPS), jnp.bfloat16),
+            pltpu.VMEM((pieces, stations, LANE), jnp.bfloat16),
+            pltpu.SemaphoreType.DMA((2,)),
+            pltpu.SemaphoreType.DMA,
+            pltpu.SemaphoreType.DMA((members,)),
+            pltpu.SemaphoreType.DMA((members,)),
+        ],
+        compiler_params=pltpu.CompilerParams(
+            collective_id=0, has_side_effects=True, vmem_limit_bytes=40 * 2**20
+        ),
+    )(raw_traces, taps, station_order.reshape(stations, 1))
+    low = low.reshape(members * pieces, stations, LANE)
     groups = jnp.concatenate([me[None].astype(jnp.int32), lax.dynamic_slice_in_dim(pairing, me, 1, 1)[:, 0]])
     planes = low.shape[0]
     grid_spec = pltpu.PrefetchScalarGridSpec(

time: 121 us -> 81.1 us (0.67)
  waiting for transfers between devices: 46.2 us -> 0 us
  Pallas kernels: 50.7 us -> 74.4 us
  between operations: 13.5 us -> 0.04 us
  starting transfers between devices: 2.37 us -> 0 us
  local copies, waits for them, and re-layouts: 8.09 us -> 6.26 us
    all_gather x1 -> x0, waiting for transfers between devices: 46.2 us -> none  [body(): low = lax.all_gather(low, 'sta', axis=0, tiled=True)]
    pallas_call x1, Pallas kernels: 1.65 us -> 25.3 us  [body(): pl.pallas_call(functools.partial(gather_kernel, members), out_shape=jax.S...]
    ppermute x1 -> x0, starting transfers between devices: 2.36 us -> none  [body(): lax.ppermute(raw_traces[:, local_time - TAPS:], 'sta', [(i, i + 1) for i...]
    unnamed x12 -> x10, local copies, waits for them, and re-layouts: 5.35 us -> 4.44 us
  transfers between devices with their start and end apart: 2 -> 0, of which waited for: 1 -> 0; matrix products, arithmetic and copies ran while one was open for 2% -> 0% of each run, Pallas kernels for 0% -> 0%
where the time goes in v2:
time: 81.1 us; the launch traced here: 80.7 us
  Pallas kernels  74.4 us (92%)
  local copies, waits for them, and re-layouts  6.26 us (8%)
    pallas_call x1, Pallas kernels, body(): pl.pallas_call(correlate_kernel, grid_spec=grid_spec, out_shape=jax.Shape...  49.1 us
    pallas_call x1, Pallas kernels, body(): pl.pallas_call(functools.partial(gather_kernel, members), out_shape=jax.S...  25.3 us
    unnamed x10, local copies, waits for them, and re-layouts  4.44 us

profile of v2, /device:TPU:0, one launch (start us, length us, event | category | flops | bytes accessed | tf_op | source)
XLA Modules:
  0.0 80.7 jit_solution(617607709698994808)
XLA Ops:
  0.0 0.0 copy-start
  0.0 0.7 copy-done
  0.7 0.2 dynamic-slice_reduce_fusion
  0.9 0.1 pad_add_fusion.groups_ref
  0.9 0.7 rev.3
  1.7 0.1 pad.4
  1.8 0.8 copy.9.order_ref
  2.6 0.0 copy-start.2
  2.6 1.0 %copy-done.2 = bf16[256,1024]{1,0:T(8,128)(2,1)S(1)} copy-done((bf16[256,1024]{1,0:T(8,128)(2,1)S(1)}, bf16[256,1024]{1,0:T(8,128)(2,1)}, u32[]{:S(2)}) %copy-start.2) | copy-done | bytes 524312
  3.6 25.3 %shard_map.82 = bf16[16,2,256,128]{3,2,1,0:T(8,128)(2,1)S(1)} custom-call(bf16[256,1024]{1,0:T(8,128)(2,1)S(1)} %copy-done.2, f32[1,768]{1,0:T(1,128)S(1)} %reshape.12.taps_ref, s32[256,1]{1,0:T(8,128)S(1)} %copy.9.order_ref), custom_call_target="tpu_custom_call" | custom-call | tf_op jit(solution)/shard_map/pallas_call | solution.py:265
  28.9 0.0 copy-start.1
  28.9 1.2 %copy-done.1 = bf16[8,256,256]{2,1,0:T(8,128)(2,1)S(1)} copy-done((bf16[8,256,256]{2,1,0:T(8,128)(2,1)S(1)}, bf16[8,256,256]{2,1,0:T(8,128)(2,1)}, u32[]{:S(2)}) %copy-start.1) | copy-done | bytes 1048600
  30.2 0.0 copy-start.3
  30.2 0.8 %copy-done.3 = bf16[256,128]{1,0:T(8,128)(2,1)S(1)} copy-done((bf16[256,128]{1,0:T(8,128)(2,1)S(1)}, bf16[256,128]{1,0:T(8,128)(2,1)}, u32[]{:S(2)}) %copy-start.3) | copy-done | bytes 65560
  31.0 0.0 copy-start.4
  31.0 0.7 copy-done.4
  31.7 49.1 %shard_map.83 = f32[4,256,256]{2,1,0:T(8,128)} custom-call(s32[16]{0:T(128)S(1)} %copy-done.4, s32[5]{0:T(128)S(1)} %pad_add_fusion.groups_ref, bf16[32,256,128]{2,1,0:T(8,128)(2,1)S(1)} %bitcast.4, bf16[8,2048,256]{2,1,0:T(8,128)(2,1)} %constant.16.clone.dft_ref, bf16[8,256,256]{2,1,0:T(8,128)(2,1)S(1)} %copy-done.1, bf16[256,128]{1,0:T(8,128)(2,1)S(1)} %copy-done.3), custom_call_target="tpu_custom_call" | custom-call | tf_op jit(solution)/shard_map/pallas_call | solution.py:303
  (1 shorter events, 0.0 us)
Async XLA Ops:
  0.0 0.7 copy-start
  2.6 1.0 %copy-start.2 = (bf16[256,1024]{1,0:T(8,128)(2,1)S(1)}, bf16[256,1024]{1,0:T(8,128)(2,1)}, u32[]{:S(2)}) copy-start(bf16[256,1024]{1,0:T(8,128)(2,1)} %raw_ref.1) | copy-start | bytes 1572868
  28.9 1.2 %copy-start.1 = (bf16[8,256,256]{2,1,0:T(8,128)(2,1)S(1)}, bf16[8,256,256]{2,1,0:T(8,128)(2,1)}, u32[]{:S(2)}) copy-start(bf16[8,256,256]{2,1,0:T(8,128)(2,1)} %constant.17.clone.lag_ref) | copy-start | bytes 3145732
  30.2 0.8 %copy-start.3 = (bf16[256,128]{1,0:T(8,128)(2,1)S(1)}, bf16[256,128]{1,0:T(8,128)(2,1)}, u32[]{:S(2)}) copy-start(bf16[256,128]{1,0:T(8,128)(2,1)} %constant.18.clone.ones_ref) | copy-start | bytes 196612
  31.0 0.7 copy-start.4

commit v3 on v2

--- a/solution.py
+++ b/solution.py
@@ -204,7 +204,7 @@
         lax.fori_loop(0, window_count, one_window, 0)
         out_ref[...] = jnp.zeros_like(out_ref)
 
-    per_chunk = 4
+    per_chunk = 8
 
     def one_chunk(n, carry):
         chunk = windows[pl.ds(pl.multiple_of(n * per_chunk * ROWS, SB), per_chunk * ROWS), :]
@@ -252,6 +252,35 @@
     lax.fori_loop(0, SB // pair, one_pair, 0)
     for r in range(ROUNDS):
         out_ref[r] += jnp.dot(cross[r], lag_ref[0], preferred_element_type=jnp.float32)
+
+
+def correlate(window_starts, groups, low, dft, lag, ones):
+    window_count = window_starts.shape[0]
+    planes = low.shape[0]
+    grid_spec = pltpu.PrefetchScalarGridSpec(
+        num_scalar_prefetch=2,
+        grid=(TILES,),
+        in_specs=[
+            pl.BlockSpec(memory_space=pl.ANY),
+            pl.BlockSpec((1, SEG, 2 * FT), lambda n, *_: (n, 0, 0)),
+            pl.BlockSpec((1, 2 * FT, LAGS), lambda n, *_: (n, 0, 0)),
+            pl.BlockSpec((2 * FT, FT), lambda n, *_: (0, 0)),
+        ],
+        out_specs=pl.BlockSpec((ROUNDS, SB * SB, LAGS), lambda n, *_: (0, 0, 0)),
+        scratch_shapes=[
+            pltpu.VMEM((planes + 1, ROWS, LANE), jnp.bfloat16),
+            pltpu.VMEM((window_count * ROWS, SEG), jnp.bfloat16),
+            pltpu.VMEM((2, window_count, ROWS, FT), jnp.float32),
+            pltpu.VMEM((ROUNDS, SB * SB, 2 * FT), jnp.bfloat16),
+            pltpu.SemaphoreType.DMA((GROUPS,)),
+        ],
+    )
+    return pl.pallas_call(
+        correlate_kernel,
+        grid_spec=grid_spec,
+        out_shape=jax.ShapeDtypeStruct((ROUNDS, SB * SB, LAGS), jnp.float32),
+        compiler_params=pltpu.CompilerParams(vmem_limit_bytes=48 * 2**20),
+    )(window_starts, groups, low, dft, lag, ones)
 
 
 def body(raw_traces, filter_taps, station_order, window_starts, pairing):
@@ -281,31 +310,7 @@
     )(raw_traces, taps, station_order.reshape(stations, 1))
     low = low.reshape(members * pieces, stations, LANE)
     groups = jnp.concatenate([me[None].astype(jnp.int32), lax.dynamic_slice_in_dim(pairing, me, 1, 1)[:, 0]])
-    planes = low.shape[0]
-    grid_spec = pltpu.PrefetchScalarGridSpec(
-        num_scalar_prefetch=2,
-        grid=(TILES,),
-        in_specs=[
-            pl.BlockSpec(memory_space=pl.ANY),
-            pl.BlockSpec((1, SEG, 2 * FT), lambda n, *_: (n, 0, 0)),
-            pl.BlockSpec((1, 2 * FT, LAGS), lambda n, *_: (n, 0, 0)),
-            pl.BlockSpec((2 * FT, FT), lambda n, *_: (0, 0)),
-        ],
-        out_specs=pl.BlockSpec((ROUNDS, SB * SB, LAGS), lambda n, *_: (0, 0, 0)),
-        scratch_shapes=[
-            pltpu.VMEM((planes + 1, ROWS, LANE), jnp.bfloat16),
-            pltpu.VMEM((window_count * ROWS, SEG), jnp.bfloat16),
-            pltpu.VMEM((2, window_count, ROWS, FT), jnp.float32),
-            pltpu.VMEM((ROUNDS, SB * SB, 2 * FT), jnp.bfloat16),
-            pltpu.SemaphoreType.DMA((GROUPS,)),
-        ],
-    )
-    correlated = pl.pallas_call(
-        correlate_kernel,
-        grid_spec=grid_spec,
-        out_shape=jax.ShapeDtypeStruct((ROUNDS, SB * SB, LAGS), jnp.float32),
-        compiler_params=pltpu.CompilerParams(vmem_limit_bytes=48 * 2**20),
-    )(
+    correlated = correlate(
         window_starts,
         groups,
         low,

time: 81.1 us -> 75.7 us (0.933)
  Pallas kernels: 74.4 us -> 69 us
    pallas_call x1, Pallas kernels: 49.1 us -> 43.7 us  [correlate(): pl.pallas_call(correlate_kernel, grid_spec=grid_spec, out_shape=jax.Shape...]
where the time goes in v3:
time: 75.7 us; the launch traced here: 75.4 us
  Pallas kernels  69 us (91%)
  local copies, waits for them, and re-layouts  6.26 us (8%)
    pallas_call x1, Pallas kernels, correlate(): pl.pallas_call(correlate_kernel, grid_spec=grid_spec, out_shape=jax.Shape...  43.7 us
    pallas_call x1, Pallas kernels, body(): pl.pallas_call(functools.partial(gather_kernel, members), out_shape=jax.S...  25.3 us
    unnamed x10, local copies, waits for them, and re-layouts  4.44 us

profile of v3, /device:TPU:0, one launch (start us, length us, event | category | flops | bytes accessed | tf_op | source)
XLA Modules:
  0.0 75.4 jit_solution(6330560864976787900)
XLA Ops:
  0.0 0.0 copy-start
  0.0 0.7 copy-done
  0.7 0.2 dynamic-slice_reduce_fusion
  0.9 0.1 pad_add_fusion.groups_ref
  0.9 0.7 rev.3
  1.7 0.1 pad.4
  1.8 0.8 %copy.9.order_ref = s32[256,1]{1,0:T(8,128)S(1)} copy(s32[256,1]{0,1:T(1,128)} %bitcast.5) | data formatting | bytes 2048 | tf_op jit(solution)/shard_map/reshape | solution.py:310
  2.6 0.0 copy-start.2
  2.6 1.0 %copy-done.2 = bf16[256,1024]{1,0:T(8,128)(2,1)S(1)} copy-done((bf16[256,1024]{1,0:T(8,128)(2,1)S(1)}, bf16[256,1024]{1,0:T(8,128)(2,1)}, u32[]{:S(2)}) %copy-start.2) | copy-done | bytes 524312
  3.6 25.3 %shard_map.82 = bf16[16,2,256,128]{3,2,1,0:T(8,128)(2,1)S(1)} custom-call(bf16[256,1024]{1,0:T(8,128)(2,1)S(1)} %copy-done.2, f32[1,768]{1,0:T(1,128)S(1)} %reshape.12.taps_ref, s32[256,1]{1,0:T(8,128)S(1)} %copy.9.order_ref), custom_call_target="tpu_custom_call" | custom-call | tf_op jit(solution)/shard_map/pallas_call | solution.py:294
  28.9 0.0 copy-start.1
  28.9 1.2 %copy-done.1 = bf16[8,256,256]{2,1,0:T(8,128)(2,1)S(1)} copy-done((bf16[8,256,256]{2,1,0:T(8,128)(2,1)S(1)}, bf16[8,256,256]{2,1,0:T(8,128)(2,1)}, u32[]{:S(2)}) %copy-start.1) | copy-done | bytes 1048600
  30.2 0.0 copy-start.3
  30.2 0.8 %copy-done.3 = bf16[256,128]{1,0:T(8,128)(2,1)S(1)} copy-done((bf16[256,128]{1,0:T(8,128)(2,1)S(1)}, bf16[256,128]{1,0:T(8,128)(2,1)}, u32[]{:S(2)}) %copy-start.3) | copy-done | bytes 65560
  31.0 0.0 copy-start.4
  31.0 0.7 copy-done.4
  31.7 43.7 %shard_map.83 = f32[4,256,256]{2,1,0:T(8,128)} custom-call(s32[16]{0:T(128)S(1)} %copy-done.4, s32[5]{0:T(128)S(1)} %pad_add_fusion.groups_ref, bf16[32,256,128]{2,1,0:T(8,128)(2,1)S(1)} %bitcast.4, bf16[8,2048,256]{2,1,0:T(8,128)(2,1)} %constant.16.clone.dft_ref, bf16[8,256,256]{2,1,0:T(8,128)(2,1)S(1)} %copy-done.1, bf16[256,128]{1,0:T(8,128)(2,1)S(1)} %copy-done.3), custom_call_target="tpu_custom_call" | custom-call | tf_op jit(solution)/shard_map/pallas_call | solution.py:278
  (1 shorter events, 0.0 us)
Async XLA Ops:
  0.0 0.7 copy-start
  2.6 1.0 %copy-start.2 = (bf16[256,1024]{1,0:T(8,128)(2,1)S(1)}, bf16[256,1024]{1,0:T(8,128)(2,1)}, u32[]{:S(2)}) copy-start(bf16[256,1024]{1,0:T(8,128)(2,1)} %raw_ref.1) | copy-start | bytes 1572868
  28.9 1.2 %copy-start.1 = (bf16[8,256,256]{2,1,0:T(8,128)(2,1)S(1)}, bf16[8,256,256]{2,1,0:T(8,128)(2,1)}, u32[]{:S(2)}) copy-start(bf16[8,256,256]{2,1,0:T(8,128)(2,1)} %constant.17.clone.lag_ref) | copy-start | bytes 3145732
  30.2 0.8 %copy-start.3 = (bf16[256,128]{1,0:T(8,128)(2,1)S(1)}, bf16[256,128]{1,0:T(8,128)(2,1)}, u32[]{:S(2)}) copy-start(bf16[256,128]{1,0:T(8,128)(2,1)} %constant.18.clone.ones_ref) | copy-start | bytes 196612
  31.0 0.7 copy-start.4
